TPU v7x, 32 devices: a whole 2x2x4 slice. The times are simulated.
32 devices in a mesh: gx: 4 (over z), gy: 8 (over y, x, core).
Axes of the slice: x: 2, y: 2, z: 4, core: 2. Of those that a mesh axis runs over, the one named last changes fastest.
Arguments:
- psi_start: float32 [6, 131072], P(None, ('gx', 'gy')), may hold values from -6 to 6
- adjoint_rhs: float32 [6, 131072], P(None, ('gx', 'gy')), may hold values from -6 to 6
- off_blocks: bfloat16 [6, 6, 6, 131072], P(None, None, None, ('gx', 'gy')), may hold values from -0.3984375 to 0.3984375
- diag_inverse: float32 [6, 6, 131072], P(None, None, ('gx', 'gy')), may hold values from -1 to 1.5, as said below
- face_nbrs: int32 [6, 131072], P(None, ('gx', 'gy')), may hold values from 0 to 8192
- halo_lists: int32 [4, 32768], P(None, ('gx', 'gy')), may hold values from 0 to 4095
- owner_lists: int32 [4, 131072], P(None, ('gx', 'gy')), may hold values from 0 to 4096, as said below
- parent_slots: int32 [2, 64, 128, 128], P(None, 'gx', 'gy'), may hold values from 0 to 16383, as said below
- parent_weights: float32 [2, 64, 128, 128], P(None, 'gx', 'gy'), may hold values from 0.2 to 1
- fine_state: float32 [6, 64, 128, 128], P(None, 'gx', 'gy'), may hold values from -6 to 6
- fine_source: float32 [6, 64, 128, 128], P(None, 'gx', 'gy'), may hold values from -6 to 6
- coupling: float32 [6, 6], replicated, may hold values from -0.375 to 0.375
Outputs:
- psi_coarse: float32 [6, 131072], P(None, ('gx', 'gy'))
- indicator: float32 [64, 128, 128], P('gx', 'gy')
Inputs may be any that keep to these rules, and one draw needn't show every extreme that they name: `owner_lists`: list k = 2 i + j of coarse partition (p, q) goes to fine partition (p - i, q - j); its live coarse cell ids fill its first slots and 4096 the rest; at most 4096 live, none where that fine partition does not exist, and one fine partition receives 4096 live from each of its four sources. `parent_slots`: each entry k * 4096 + m names a live slot m of list k received by this fine partition. `diag_inverse`: diagonal entries of each block are positive; each off-diagonal entry is at most 0.6 times its column's diagonal entry in magnitude.
All inputs are finite; a program needn't handle non-finite values.
Results may differ from a plain program's by a relative error of at most 0.0003.
Values sent between devices are 32-bit elements; how exact they have to be, the bound alone decides.
A program may use at most 128 MiB of HBM per device.

v0:
```python
import jax
import jax.numpy as jnp
from jax import lax
from jax.sharding import PartitionSpec as P

SWEEPS = 2


def passed_along(value, axis, by):
    peers = lax.axis_size(axis)
    pairs = [(i, i + by) for i in range(peers) if 0 <= i + by < peers]
    return lax.ppermute(value, axis, pairs)


def padded_2(cells, sides, width):
    for axis, dim in sides:
        count = lax.axis_size(axis)
        ends = count - 1
        head = lax.slice_in_dim(cells, 0, width, axis=dim)
        tail = lax.slice_in_dim(cells, cells.shape[dim] - width, cells.shape[dim], axis=dim)
        cells = jnp.concatenate(
            [
                lax.ppermute(tail, axis, [(i, (i + 1) % count) for i in range(ends)]),
                cells,
                lax.ppermute(head, axis, [((i + 1) % count, i) for i in range(ends)]),
            ],
            axis=dim,
        )
    return cells


def extend(psi, halo_lists):
    packed = psi[:, halo_lists]
    recv_zero = passed_along(packed[:, 0], "gx", 1)
    recv_one = passed_along(packed[:, 1], "gx", -1)
    recv_two = passed_along(packed[:, 2], "gy", 1)
    recv_three = passed_along(packed[:, 3], "gy", -1)
    empty = jnp.zeros((psi.shape[0], 1), jnp.float32)
    return jnp.concatenate([psi, recv_zero, recv_one, recv_two, recv_three, empty], axis=1)


def fine_stencil(fine_state, fine_source, coupling):
    grown = padded_2(fine_state, (("gx", 1), ("gy", 2)), 1)
    padfine = jnp.pad(grown, ((0, 0), (0, 0), (0, 0), (1, 1)))
    beside = padfine[:, 2:, 1:-1, 1:-1] + padfine[:, :-2, 1:-1, 1:-1]
    beside = beside + padfine[:, 1:-1, 2:, 1:-1] + padfine[:, 1:-1, :-2, 1:-1]
    beside = beside + padfine[:, 1:-1, 1:-1, 2:] + padfine[:, 1:-1, 1:-1, :-2]
    lap = 6.0 * fine_state - beside
    return jnp.einsum("ck,kabz->cabz", coupling, lap, precision=lax.Precision.HIGHEST) + fine_source


def on_device(
    psi_start,
    adjoint_rhs,
    off_blocks,
    diag_inverse,
    face_nbrs,
    halo_lists,
    owner_lists,
    parent_slots,
    parent_weights,
    fine_state,
    fine_source,
    coupling,
):
    comps = psi_start.shape[0]
    faces = off_blocks.shape[0]
    fine_residual = fine_stencil(fine_state, fine_source, coupling)
    psi = psi_start
    for sweep in range(SWEEPS):
        ext = extend(psi, halo_lists)
        acc = adjoint_rhs
        for face in range(faces):
            values = ext[:, face_nbrs[face]]
            for row in range(comps):
                acc = acc - off_blocks[face, row].astype(jnp.float32) * values[row][None]
        fresh = jnp.zeros(psi.shape, jnp.float32)
        for row in range(comps):
            fresh = fresh + diag_inverse[row] * acc[row][None]
        psi = fresh
    size_gy = lax.axis_size("gy")
    padded = jnp.concatenate([psi, jnp.zeros((comps, 1), jnp.float32)], axis=1)
    packed = padded[:, owner_lists]
    beside = passed_along(packed[:, 1], ("gx", "gy"), -1)
    below = passed_along(packed[:, 2], ("gx", "gy"), -size_gy)
    corner = passed_along(packed[:, 3], ("gx", "gy"), -size_gy - 1)
    pieces = [packed[:, 0], beside, below, corner]
    received = jnp.concatenate(pieces, axis=1)
    fine_shape = fine_state.shape
    flat_first = parent_slots[0].reshape(-1)
    flat_second = parent_slots[1].reshape(-1)
    weight_first = parent_weights[0].reshape(-1)
    weight_second = parent_weights[1].reshape(-1)
    fine_psi = (
        weight_first[None] * received[:, flat_first]
        + weight_second[None] * received[:, flat_second]
    )
    fine_psi = fine_psi.reshape(fine_shape)
    indicator = jnp.sum(fine_psi * fine_residual, axis=0)
    return (psi, indicator)


def solution(mesh):
    placed = (
        P(None, ("gx", "gy")),
        P(None, ("gx", "gy")),
        P(None, None, None, ("gx", "gy")),
        P(None, None, ("gx", "gy")),
        P(None, ("gx", "gy")),
        P(None, ("gx", "gy")),
        P(None, ("gx", "gy")),
        P(None, "gx", "gy", None),
        P(None, "gx", "gy", None),
        P(None, "gx", "gy", None),
        P(None, "gx", "gy", None),
        P(),
    )
    return jax.shard_map(
        on_device,
        mesh=mesh,
        in_specs=placed,
        out_specs=(P(None, ("gx", "gy")), P("gx", "gy", None)),
        check_vma=False,
    )
```

profile of v0, /device:TPU:1, one launch (start us, length us, event | category | flops | bytes accessed | tf_op | source)
XLA Modules:
  0.0 707.7 jit_solution(18135189747634682075)
XLA Ops:
  2.2 14.1 %gather_fusion = f32[4096,6]{1,0:T(8,128)} fusion(f32[6,4096]{0,1:T(8,128)S(1)} %copy.99, s32[4096]{0:T(1024)S(1)} %bitcast_clamp_fusion), kind=kCustom, calls=%fused_computation | custom fusion | bytes 212992 | tf_op jit(solution)/shard_map/gather | solution.py:33
  16.3 2.9 slice_bitcast_fusion.4
  19.2 4.8 collective-permute-start
  25.4 4.0 collective-permute-start.2
  32.1 4.4 collective-permute-start.12
  60.9 13.0 %gather_fusion.6 = f32[4096,6]{1,0:T(8,128)S(1)} fusion(f32[6,8193]{0,1:T(8,128)} %dynamic-update-slice.14, s32[4096]{0:T(1024)S(1)} %get-tuple-element.130), kind=kCustom, calls=%fused_computation.6 | custom fusion | bytes 212992 | tf_op jit(solution)/shard_map/gather | solution.py:74
  73.8 6.0 slice_reduce_fusion.41
  79.9 13.0 %gather_fusion.5 = f32[4096,6]{1,0:T(8,128)S(1)} fusion(f32[6,8193]{0,1:T(8,128)} %dynamic-update-slice.14, s32[4096]{0:T(1024)S(1)} %get-tuple-element.131), kind=kCustom, calls=%fused_computation.5 | custom fusion | bytes 212992 | tf_op jit(solution)/shard_map/gather | solution.py:74
  92.9 6.0 slice_reduce_fusion.47
  98.9 13.5 %gather_fusion.4 = f32[4096,6]{1,0:T(8,128)S(1)} fusion(f32[6,8193]{0,1:T(8,128)} %dynamic-update-slice.14, s32[4096]{0:T(1024)S(1)} %get-tuple-element.132), kind=kCustom, calls=%fused_computation.4 | custom fusion | bytes 212992 | tf_op jit(solution)/shard_map/gather | solution.py:74
  112.4 6.0 slice_reduce_fusion.53
  118.5 13.0 %gather_fusion.3 = f32[4096,6]{1,0:T(8,128)S(1)} fusion(f32[6,8193]{0,1:T(8,128)} %dynamic-update-slice.14, s32[4096]{0:T(1024)S(1)} %get-tuple-element.133), kind=kCustom, calls=%fused_computation.3 | custom fusion | bytes 212992 | tf_op jit(solution)/shard_map/gather | solution.py:74
  131.4 6.0 slice_reduce_fusion.59
  137.5 13.2 %gather_fusion.2 = f32[4096,6]{1,0:T(8,128)S(1)} fusion(f32[6,8193]{0,1:T(8,128)} %dynamic-update-slice.14, s32[4096]{0:T(1024)S(1)} %get-tuple-element.134), kind=kCustom, calls=%fused_computation.2 | custom fusion | bytes 212992 | tf_op jit(solution)/shard_map/gather | solution.py:74
  150.6 6.0 slice_reduce_fusion.65
  156.7 13.0 %gather_fusion.1 = f32[4096,6]{1,0:T(8,128)S(1)} fusion(f32[6,8193]{0,1:T(8,128)} %dynamic-update-slice.14, s32[4096]{0:T(1024)S(1)} %get-tuple-element.135), kind=kCustom, calls=%fused_computation.1 | custom fusion | bytes 212992 | tf_op jit(solution)/shard_map/gather | solution.py:74
  169.7 6.0 slice_reduce_fusion.71
  175.8 2.4 fusion.79
  178.3 5.8 constant_dynamic-update-slice_fusion.9
  184.1 14.2 %gather_fusion.7 = f32[4096,6]{1,0:T(8,128)} fusion(f32[6,4096]{0,1:T(8,128)S(1)} %get-tuple-element.85, s32[4096]{0:T(1024)S(1)} %bitcast_clamp_fusion), kind=kCustom, calls=%fused_computation.7 | custom fusion | bytes 212992 | tf_op jit(solution)/shard_map/gather | solution.py:33
  200.0 4.0 collective-permute-start.4
  206.1 4.5 collective-permute-start.6
  210.6 3.9 collective-permute-done.4
  217.2 2.1 collective-permute-done.5
  221.0 5.0 collective-permute-done.7
  228.1 16.4 %gather_fusion.13 = f32[4096,6]{1,0:T(8,128)} fusion(f32[6,8193]{0,1:T(8,128)} %dynamic-update-slice.8, s32[4096]{0:T(1024)S(1)} %get-tuple-element.130), kind=kCustom, calls=%fused_computation.13 | custom fusion | bytes 212992 | tf_op jit(solution)/shard_map/gather | solution.py:74
  244.5 16.3 %gather_fusion.12 = f32[4096,6]{1,0:T(8,128)} fusion(f32[6,8193]{0,1:T(8,128)} %dynamic-update-slice.8, s32[4096]{0:T(1024)S(1)} %get-tuple-element.131), kind=kCustom, calls=%fused_computation.12 | custom fusion | bytes 212992 | tf_op jit(solution)/shard_map/gather | solution.py:74
  260.8 16.4 %gather_fusion.11 = f32[4096,6]{1,0:T(8,128)} fusion(f32[6,8193]{0,1:T(8,128)} %dynamic-update-slice.8, s32[4096]{0:T(1024)S(1)} %get-tuple-element.132), kind=kCustom, calls=%fused_computation.11 | custom fusion | bytes 212992 | tf_op jit(solution)/shard_map/gather | solution.py:74
  277.2 16.4 %gather_fusion.10 = f32[4096,6]{1,0:T(8,128)} fusion(f32[6,8193]{0,1:T(8,128)} %dynamic-update-slice.8, s32[4096]{0:T(1024)S(1)} %get-tuple-element.133), kind=kCustom, calls=%fused_computation.10 | custom fusion | bytes 212992 | tf_op jit(solution)/shard_map/gather | solution.py:74
  293.5 16.4 %gather_fusion.9 = f32[4096,6]{1,0:T(8,128)} fusion(f32[6,8193]{0,1:T(8,128)} %dynamic-update-slice.8, s32[4096]{0:T(1024)S(1)} %get-tuple-element.134), kind=kCustom, calls=%fused_computation.9 | custom fusion | bytes 212992 | tf_op jit(solution)/shard_map/gather | solution.py:74
  309.9 13.4 %gather_fusion.8 = f32[4096,6]{1,0:T(8,128)S(1)} fusion(f32[6,8193]{0,1:T(8,128)} %dynamic-update-slice.8, s32[4096]{0:T(1024)S(1)} %get-tuple-element.135), kind=kCustom, calls=%fused_computation.8 | custom fusion | bytes 212992 | tf_op jit(solution)/shard_map/gather | solution.py:74
  323.3 11.9 %slice_reduce_fusion.5 = (f32[4096]{0:T(1024)S(1)}, f32[4096]{0:T(1024)S(1)}, f32[4096]{0:T(1024)S(1)}, f32[4096]{0:T(1024)S(1)}, f32[4096]{0:T(1024)S(1)}, /*index=5*/f32[4096]{0:T(1024)S(1)}) fusion(f32[6,4096]{0,1:T(8,128)} %bitcast.321), kind=kLoop, calls=%fused_computation.27 | loop fusion | bytes 196608 | tf_op jit(solution)/shard_map/slice | solution.py:76
  335.2 6.0 slice_reduce_fusion.11
  341.3 6.2 slice_reduce_fusion.17
  347.5 6.0 slice_reduce_fusion.23
  353.5 6.2 slice_reduce_fusion.29
  359.8 6.0 slice_reduce_fusion.35
  369.8 3.6 collective-permute-start.14
  373.5 4.2 fusion.2
  379.2 56.0 %gather_fusion.14 = f32[16384,6]{1,0:T(8,128)} fusion(f32[6,4097]{0,1:T(8,128)} %concatenate.32, s32[16384]{0:T(1024)S(1)} %broadcast_clamp_fusion.2), kind=kCustom, calls=%fused_computation.14 | custom fusion | bytes 851968 | tf_op jit(solution)/shard_map/gather | solution.py:83
  435.3 5.4 copy.105
  451.0 3.5 collective-permute-done.9
  454.6 5.6 copy.106
  460.1 111.6 %gather_fusion.16 = f32[32768,6]{1,0:T(8,128)} fusion(f32[6,16384]{0,1:T(8,128)} %copy.106, s32[32768]{0:T(1024)S(1)} %copy-done.21), kind=kCustom, calls=%fused_computation.16 | custom fusion | bytes 1703936 | tf_op jit(solution)/shard_map/gather | solution.py:96
  571.7 10.0 %copy.111 = f32[6,16,16,128]{3,0,2,1:T(8,128)S(1)} copy(f32[6,16,16,128]{0,3,2,1:T(8,128)} %bitcast.329) | data formatting | bytes 1572864 | tf_op jit(solution)/shard_map/gather | solution.py:96
  581.7 111.6 %gather_fusion.15 = f32[32768,6]{1,0:T(8,128)} fusion(f32[6,16384]{0,1:T(8,128)} %copy.106, s32[32768]{0:T(1024)S(1)} %copy-done.22), kind=kCustom, calls=%fused_computation.15 | custom fusion | bytes 1703936 | tf_op jit(solution)/shard_map/gather | solution.py:95
  693.3 10.0 %copy.108 = f32[6,16,16,128]{3,0,2,1:T(8,128)S(1)} copy(f32[6,16,16,128]{0,3,2,1:T(8,128)} %bitcast.328) | data formatting | bytes 1572864 | tf_op jit(solution)/shard_map/gather | solution.py:95
  703.4 4.1 fusion.13
  (148 shorter events, 55.9 us)
Async XLA Ops:
  0.6 702.7 %copy-start = (f32[6,6]{1,0:T(8,128)S(1)}, f32[6,6]{1,0:T(8,128)}, u32[]{:S(2)}) copy-start(f32[6,6]{1,0:T(8,128)} %param.23) | copy-start | bytes 436
  19.2 33.3 %collective-permute-start = (f32[6,1024]{0,1:T(8,128)}, f32[6,1024]{0,1:T(8,128)}, u32[]{:S(2)}, u32[]{:S(2)}) collective-permute-start(f32[6,1024]{0,1:T(8,128)} %get-tuple-element.93), channel_id=1, source_target_pairs={{0,8},{8,16},{16,24},{1,9},{9,17},{17,25},{2,10},{10,18},{18,26},{... | collective-permute-start | bytes 73736 | tf_op jit(solution)/shard_map/ppermute | solution.py:12
  24.1 31.9 %collective-permute-start.1 = (f32[6,1024]{0,1:T(8,128)}, f32[6,1024]{0,1:T(8,128)}, u32[]{:S(2)}, u32[]{:S(2)}) collective-permute-start(f32[6,1024]{0,1:T(8,128)} %get-tuple-element.92), channel_id=1, source_target_pairs={{8,0},{16,8},{24,16},{9,1},{17,9},{25,17},{10,2},{18,10},{26,18},{... | collective-permute-start | bytes 73736 | tf_op jit(solution)/shard_map/ppermute | solution.py:12
  25.4 32.5 %collective-permute-start.2 = (f32[6,1024]{0,1:T(8,128)}, f32[6,1024]{0,1:T(8,128)S(1)}, u32[]{:S(2)}, u32[]{:S(2)}) collective-permute-start(f32[6,1024]{0,1:T(8,128)} %get-tuple-element.91), channel_id=1, source_target_pairs={{0,1},{1,2},{2,3},{3,4},{4,5},{5,6},{6,7},{8,9},{9,10},{10,11},{11... | collective-permute-start | bytes 73736 | tf_op jit(solution)/shard_map/ppermute | solution.py:12
  29.3 29.4 %collective-permute-start.3 = (f32[6,1024]{0,1:T(8,128)}, f32[6,1024]{0,1:T(8,128)S(1)}, u32[]{:S(2)}, u32[]{:S(2)}) collective-permute-start(f32[6,1024]{0,1:T(8,128)} %get-tuple-element.90), channel_id=1, source_target_pairs={{1,0},{2,1},{3,2},{4,3},{5,4},{6,5},{7,6},{9,8},{10,9},{11,10},{12... | collective-permute-start | bytes 73736 | tf_op jit(solution)/shard_map/ppermute | solution.py:12
  32.1 5.9 copy-start.20
  32.1 6.0 copy-start.36
  32.1 6.1 copy-start.37
  32.1 334.5 %collective-permute-start.12 = (f32[6,1,16,128]{3,2,1,0:T(8,128)S(1)}, f32[6,1,16,128]{3,2,1,0:T(8,128)S(1)}, u32[]{:S(2)}, u32[]{:S(2)}) collective-permute-start(f32[6,1,16,128]{3,2,1,0:T(8,128)S(1)} %get-tuple-element.97), channel_id=1, source_target_pairs={{0,8},{8,16},{16,24},{1,9},{9,17},{17,25},{2,10},{10,18},{18,26},{... | collective-permute-start | bytes 147464 | tf_op jit(solution)/shard_map/ppermute | solution.py:23
  52.5 314.5 %collective-permute-start.11 = (f32[6,1,16,128]{3,2,1,0:T(8,128)S(1)}, f32[6,1,16,128]{3,2,1,0:T(8,128)S(1)}, u32[]{:S(2)}, u32[]{:S(2)}) collective-permute-start(f32[6,1,16,128]{3,2,1,0:T(8,128)S(1)} %get-tuple-element.96), channel_id=1, source_target_pairs={{8,0},{16,8},{24,16},{9,1},{17,9},{25,17},{10,2},{18,10},{26,18},{... | collective-permute-start | bytes 147464 | tf_op jit(solution)/shard_map/ppermute | solution.py:25
  169.7 6.1 copy-start.23
  169.7 8.6 %copy-start.7 = (f32[1,6,4096]{1,2,0:T(8,128)S(1)}, f32[1,6,4096]{1,2,0:T(8,128)}, u32[]{:S(2)}) copy-start(f32[1,6,4096]{1,2,0:T(8,128)} %copy.124) | copy-start | bytes 294916
  169.7 8.6 %copy-start.9 = (f32[1,6,4096]{1,2,0:T(8,128)S(1)}, f32[1,6,4096]{1,2,0:T(8,128)}, u32[]{:S(2)}) copy-start(f32[1,6,4096]{1,2,0:T(8,128)} %copy.123) | copy-start | bytes 294916
  169.7 8.6 %copy-start.11 = (f32[1,6,4096]{1,2,0:T(8,128)S(1)}, f32[1,6,4096]{1,2,0:T(8,128)}, u32[]{:S(2)}) copy-start(f32[1,6,4096]{1,2,0:T(8,128)} %copy.122) | copy-start | bytes 294916
  169.7 8.6 %copy-start.13 = (f32[1,6,4096]{1,2,0:T(8,128)S(1)}, f32[1,6,4096]{1,2,0:T(8,128)}, u32[]{:S(2)}) copy-start(f32[1,6,4096]{1,2,0:T(8,128)} %copy.121) | copy-start | bytes 294916
  169.7 8.6 %copy-start.15 = (f32[1,6,4096]{1,2,0:T(8,128)S(1)}, f32[1,6,4096]{1,2,0:T(8,128)}, u32[]{:S(2)}) copy-start(f32[1,6,4096]{1,2,0:T(8,128)} %copy.120) | copy-start | bytes 294916
  198.3 5.7 copy-start.28
  200.0 14.4 %collective-permute-start.4 = (f32[6,1024]{0,1:T(8,128)S(1)}, f32[6,1024]{0,1:T(8,128)S(1)}, u32[]{:S(2)}, u32[]{:S(2)}) collective-permute-start(f32[6,1024]{0,1:T(8,128)S(1)} %get-tuple-element.89), channel_id=1, source_target_pairs={{0,8},{8,16},{16,24},{1,9},{9,17},{17,25},{2,10},{10,18},{18,26},{... | collective-permute-start | bytes 73736 | tf_op jit(solution)/shard_map/ppermute | solution.py:12
  204.8 14.5 %collective-permute-start.5 = (f32[6,1024]{0,1:T(8,128)S(1)}, f32[6,1024]{0,1:T(8,128)S(1)}, u32[]{:S(2)}, u32[]{:S(2)}) collective-permute-start(f32[6,1024]{0,1:T(8,128)S(1)} %get-tuple-element.88), channel_id=1, source_target_pairs={{8,0},{16,8},{24,16},{9,1},{17,9},{25,17},{10,2},{18,10},{26,18},{... | collective-permute-start | bytes 73736 | tf_op jit(solution)/shard_map/ppermute | solution.py:12
  206.1 14.1 %collective-permute-start.6 = (f32[6,1024]{0,1:T(8,128)S(1)}, f32[6,1024]{0,1:T(8,128)S(1)}, u32[]{:S(2)}, u32[]{:S(2)}) collective-permute-start(f32[6,1024]{0,1:T(8,128)S(1)} %get-tuple-element.87), channel_id=1, source_target_pairs={{0,1},{1,2},{2,3},{3,4},{4,5},{5,6},{6,7},{8,9},{9,10},{10,11},{11... | collective-permute-start | bytes 73736 | tf_op jit(solution)/shard_map/ppermute | solution.py:12
  214.4 11.5 %collective-permute-start.7 = (f32[6,1024]{0,1:T(8,128)S(1)}, f32[6,1024]{0,1:T(8,128)S(1)}, u32[]{:S(2)}, u32[]{:S(2)}) collective-permute-start(f32[6,1024]{0,1:T(8,128)S(1)} %get-tuple-element.86), channel_id=1, source_target_pairs={{1,0},{2,1},{3,2},{4,3},{5,4},{6,5},{7,6},{9,8},{10,9},{11,10},{12... | collective-permute-start | bytes 73736 | tf_op jit(solution)/shard_map/ppermute | solution.py:12
  323.3 11.9 %copy-start.4 = (f32[4096,6]{1,0:T(8,128)S(1)}, f32[4096,6]{1,0:T(8,128)}, u32[]{:S(2)}) copy-start(f32[4096,6]{1,0:T(8,128)} %gather_fusion.12) | copy-start | bytes 294916
  335.2 6.1 copy-start.3
  341.3 6.2 copy-start.2
  347.5 6.1 copy-start.1
  359.8 6.1 copy-start.17
  359.8 13.6 %copy-start.10 = (f32[1,6,4096]{1,2,0:T(8,128)S(1)}, f32[1,6,4096]{1,2,0:T(8,128)}, u32[]{:S(2)}) copy-start(f32[1,6,4096]{1,2,0:T(8,128)} %copy.123) | copy-start | bytes 294916
  359.8 13.6 %copy-start.12 = (f32[1,6,4096]{1,2,0:T(8,128)S(1)}, f32[1,6,4096]{1,2,0:T(8,128)}, u32[]{:S(2)}) copy-start(f32[1,6,4096]{1,2,0:T(8,128)} %copy.122) | copy-start | bytes 294916
  359.8 13.6 %copy-start.14 = (f32[1,6,4096]{1,2,0:T(8,128)S(1)}, f32[1,6,4096]{1,2,0:T(8,128)}, u32[]{:S(2)}) copy-start(f32[1,6,4096]{1,2,0:T(8,128)} %copy.121) | copy-start | bytes 294916
  359.8 13.6 %copy-start.16 = (f32[1,6,4096]{1,2,0:T(8,128)S(1)}, f32[1,6,4096]{1,2,0:T(8,128)}, u32[]{:S(2)}) copy-start(f32[1,6,4096]{1,2,0:T(8,128)} %copy.120) | copy-start | bytes 294916
  365.9 7.6 %copy-start.6 = (f32[1,6,4096]{1,2,0:T(8,128)S(1)}, f32[1,6,4096]{1,2,0:T(8,128)}, u32[]{:S(2)}) copy-start(f32[1,6,4096]{1,2,0:T(8,128)} %copy.125) | copy-start | bytes 294916
  365.9 7.6 %copy-start.8 = (f32[1,6,4096]{1,2,0:T(8,128)S(1)}, f32[1,6,4096]{1,2,0:T(8,128)}, u32[]{:S(2)}) copy-start(f32[1,6,4096]{1,2,0:T(8,128)} %copy.124) | copy-start | bytes 294916
  366.6 11.1 %copy-start.29 = (f32[6,1,16,128]{3,2,1,0:T(8,128)}, f32[6,1,16,128]{3,2,1,0:T(8,128)S(1)}, u32[]{:S(2)}) copy-start(f32[6,1,16,128]{3,2,1,0:T(8,128)S(1)} %collective-permute-done.12) | copy-start | bytes 147460
  367.1 10.6 %copy-start.31 = (f32[6,1,16,128]{3,2,1,0:T(8,128)}, f32[6,1,16,128]{3,2,1,0:T(8,128)S(1)}, u32[]{:S(2)}) copy-start(f32[6,1,16,128]{3,2,1,0:T(8,128)S(1)} %collective-permute-done.11) | copy-start | bytes 147460
  367.9 79.5 %collective-permute-start.13 = (f32[6,18,1,128]{3,2,1,0:T(1,128)}, f32[6,18,1,128]{3,2,1,0:T(1,128)}, u32[]{:S(2)}, u32[]{:S(2)}) collective-permute-start(f32[6,18,1,128]{3,2,1,0:T(1,128)} %get-tuple-element.95), channel_id=1, source_target_pairs={{1,0},{2,1},{3,2},{4,3},{5,4},{6,5},{7,6},{9,8},{10,9},{11,10},{12... | collective-permute-start | bytes 165896 | tf_op jit(solution)/shard_map/ppermute | solution.py:25
  369.8 77.6 %collective-permute-start.14 = (f32[6,18,1,128]{3,2,1,0:T(1,128)}, f32[6,18,1,128]{3,2,1,0:T(1,128)}, u32[]{:S(2)}, u32[]{:S(2)}) collective-permute-start(f32[6,18,1,128]{3,2,1,0:T(1,128)} %get-tuple-element.94), channel_id=1, source_target_pairs={{0,1},{1,2},{2,3},{3,4},{4,5},{5,6},{6,7},{8,9},{9,10},{10,11},{11... | collective-permute-start | bytes 165896 | tf_op jit(solution)/shard_map/ppermute | solution.py:23
  441.4 4.0 copy-start.33
  442.7 6.8 copy-start.19
  442.7 6.8 copy-start.30
  442.7 6.8 copy-start.32
  442.7 8.3 %collective-permute-start.10 = (f32[6,4096]{1,0:T(8,128)S(1)}, f32[6,4096]{1,0:T(8,128)S(1)}, u32[]{:S(2)}, u32[]{:S(2)}) collective-permute-start(f32[6,4096]{1,0:T(8,128)S(1)} %copy-done.35), channel_id=1, source_target_pairs={{9,0},{10,1},{11,2},{12,3},{13,4},{14,5},{15,6},{16,7},{17,8},{18,... | collective-permute-start | bytes 294920 | tf_op jit(solution)/shard_map/ppermute | solution.py:12
  444.2 10.3 %collective-permute-start.9 = (f32[6,4096]{1,0:T(8,128)S(1)}, f32[6,4096]{1,0:T(8,128)S(1)}, u32[]{:S(2)}, u32[]{:S(2)}) collective-permute-start(f32[6,4096]{1,0:T(8,128)S(1)} %copy-done.34), channel_id=1, source_target_pairs={{8,0},{9,1},{10,2},{11,3},{12,4},{13,5},{14,6},{15,7},{16,8},{17,9... | collective-permute-start | bytes 294920 | tf_op jit(solution)/shard_map/ppermute | solution.py:12
  445.5 9.0 %collective-permute-start.8 = (f32[6,4096]{1,0:T(8,128)S(1)}, f32[6,4096]{1,0:T(8,128)S(1)}, u32[]{:S(2)}, u32[]{:S(2)}) collective-permute-start(f32[6,4096]{1,0:T(8,128)S(1)} %copy-done.33), channel_id=1, source_target_pairs={{1,0},{2,1},{3,2},{4,3},{5,4},{6,5},{7,6},{8,7},{9,8},{10,9},{11,1... | collective-permute-start | bytes 294920 | tf_op jit(solution)/shard_map/ppermute | solution.py:12
  449.5 5.0 copy-start.24
  454.5 5.6 copy-start.21
  571.7 10.0 %copy-start.22 = (s32[32768]{0:T(1024)S(1)}, s32[32768]{0:T(1024)}, u32[]{:S(2)}) copy-start(s32[32768]{0:T(1024)} %broadcast_clamp_fusion.1) | copy-start | bytes 393220
  693.3 10.0 %copy-start.25 = (f32[16,16,128]{2,1,0:T(8,128)S(1)}, f32[16,16,128]{2,1,0:T(8,128)}, u32[]{:S(2)}) copy-start(f32[16,16,128]{2,1,0:T(8,128)} %get-tuple-element.108) | copy-start | bytes 393220
  693.3 10.0 %copy-start.26 = (f32[16,16,128]{2,1,0:T(8,128)S(1)}, f32[16,16,128]{2,1,0:T(8,128)}, u32[]{:S(2)}) copy-start(f32[16,16,128]{2,1,0:T(8,128)} %get-tuple-element.109) | copy-start | bytes 393220
  (6 other events, 10.2 us)
where the time goes:
time: 713 us; the launch traced here: 708 us
  local copies, waits for them, and re-layouts  629 us (88%)
  starting transfers between devices  39.9 us (6%)
  other arithmetic  18.3 us (3%)
  waiting for transfers between devices  14.5 us (2%)
    gather x12, local copies, waits for them, and re-layouts, on_device(): values = ext[:, face_nbrs[face]]  174 us
    gather x2, local copies, waits for them, and re-layouts, on_device(): received[:, flat_first]  122 us
    gather x2, local copies, waits for them, and re-layouts, on_device(): received[:, flat_second]  122 us
    slice x12, local copies, waits for them, and re-layouts, on_device(): acc = acc - off_blocks[face, row].astype(jnp.float32) * values[row][None]  78.6 us
    gather x2, local copies, waits for them, and re-layouts, on_device(): packed = padded[:, owner_lists]  61.4 us
    ppermute x11, starting transfers between devices, passed_along(): return lax.ppermute(value, axis, pairs)  28.3 us
    gather x2, local copies, waits for them, and re-layouts, extend(): packed = psi[:, halo_lists]  28.2 us
    unnamed x98, local copies, waits for them, and re-layouts  26.3 us
  transfers between devices with their start and end apart: 15, of which 4 were waited for; matrix products, arithmetic and copies ran while one was open for 53% of the time, Pallas kernels for 0%

commit v1 on v0

v1 whole, which is shorter than its diff:
```python
import functools

import jax
import jax.numpy as jnp
from jax import lax
from jax.experimental import pallas as pl
from jax.experimental.pallas import tpu as pltpu
from jax.sharding import PartitionSpec as P

SWEEPS = 2
LANES = 128
MESH = pl.DeviceIdType.MESH


def lane_take(table, lanes):
    return jnp.take_along_axis(table, lanes, axis=1, mode="promise_in_bounds")


def to_rows(src, dst):
    lists, cells = src.shape
    for k in range(lists):
        for j in range(cells // LANES):
            dst[k, j : j + 1, :] = src[k : k + 1, j * LANES : (j + 1) * LANES]


def pick(indices, totals, segments, comps, unroll=8):
    lanes = [index & (LANES - 1) for index in indices]
    rows = [index >> 7 for index in indices]
    for first, count, load in segments:

        def step(j, totals):
            values = [jnp.broadcast_to(load(c, j), (8, LANES)) for c in range(comps)]
            out = []
            for u in range(len(indices)):
                here = rows[u] == first + j
                for c in range(comps):
                    out.append(jnp.where(here, lane_take(values[c], lanes[u]), totals[u * comps + c]))
            return tuple(out)

        totals = lax.fori_loop(0, count, step, tuple(totals), unroll=min(unroll, count))
    return totals


def zeros_8(count):
    return [jnp.zeros((8, LANES), jnp.float32) for _ in range(count)]


def kernel(
    peers,
    psi_start,
    rhs,
    off,
    diag,
    nbrs,
    halos,
    owners,
    slots,
    weights,
    fine,
    source,
    coupling,
    psi_out,
    indicator,
    psi_mid,
    nbr_rows,
    halo_rows,
    owner_rows,
    picked,
    halo_out,
    halo_in,
    owner_out,
    owner_in,
    grown,
    side_out,
    side_in,
    residual,
    send_sem,
    recv_sem,
):
    comps, cells = psi_start.shape
    faces = off.shape[0]
    blocks = cells // LANES
    halo_blocks = halo_rows.shape[1]
    _, fa, fb, _ = fine.shape
    n_x, n_y = peers
    p, q = lax.axis_index("gx"), lax.axis_index("gy")

    def exists(dx, dy):
        ok = None
        for pos, by, n in ((p, dx, n_x), (q, dy, n_y)):
            if by:
                one = (pos + by >= 0) & (pos + by < n)
                ok = one if ok is None else ok & one
        return ok

    halo_in[...] = jnp.zeros_like(halo_in)
    owner_in[...] = jnp.zeros_like(owner_in)
    side_in[...] = jnp.zeros_like(side_in)
    grown[:, 0:1, :, :] = jnp.zeros((comps, 1, fb + 16, LANES), jnp.float32)
    grown[:, fa + 1 : fa + 2, :, :] = jnp.zeros((comps, 1, fb + 16, LANES), jnp.float32)

    around = ((1, 0), (-1, 0), (0, 1), (0, -1))
    barrier = pltpu.get_barrier_semaphore()
    for dx, dy in around + ((-1, -1), (1, 1)):
        @pl.when(exists(dx, dy))
        def _():
            pl.semaphore_signal(barrier, inc=1, device_id=(p + dx, q + dy), device_id_type=MESH)
    side_out[0] = fine[:, :, 0, :]
    side_out[1] = fine[:, :, fb - 1, :]
    met = [jnp.where(exists(dx, dy), 1, 0) for dx, dy in around + ((-1, -1), (1, 1))]
    pl.semaphore_wait(barrier, sum(met[1:], met[0]))

    def remote(src, dst, number, dx, dy):
        return (
            pltpu.make_async_remote_copy(
                src_ref=src,
                dst_ref=dst,
                send_sem=send_sem.at[number],
                recv_sem=recv_sem.at[number],
                device_id=(p + dx, q + dy),
                device_id_type=MESH,
            ),
            dx,
            dy,
        )

    def start(copies):
        for copy, dx, dy in copies:
            @pl.when(exists(dx, dy))
            def _():
                copy.start()

    def arrive(copies):
        for copy, dx, dy in copies:
            @pl.when(exists(-dx, -dy))
            def _():
                copy.wait_recv()

    def leave(copies):
        for copy, dx, dy in copies:
            @pl.when(exists(dx, dy))
            def _():
                copy.wait_send()

    fine_copies = [
        remote(fine.at[:, fa - 1], grown.at[:, 0, 8 : 8 + fb, :], 8, 1, 0),
        remote(fine.at[:, 0], grown.at[:, fa + 1, 8 : 8 + fb, :], 9, -1, 0),
        remote(side_out.at[1], side_in.at[0], 10, 0, 1),
        remote(side_out.at[0], side_in.at[1], 11, 0, -1),
    ]
    start(fine_copies)

    to_rows(halos, halo_rows)

    def own(ref):
        return lambda c, j: ref[c : c + 1, pl.ds(pl.multiple_of(j * LANES, LANES), LANES)]

    every = []
    for sweep in range(SWEEPS):
        psi = psi_start if sweep == 0 else psi_mid
        fresh = psi_mid if sweep == 0 else psi_out
        for d in range(4):
            sums = pick([halo_rows[d]], zeros_8(comps), [(0, blocks, own(psi))], comps)
            for c in range(comps):
                halo_out[sweep, d, c] = sums[c]
        copies = [
            remote(halo_out.at[sweep, d], halo_in.at[sweep, d], sweep * 4 + d, *around[d])
            for d in range(4)
        ]
        start(copies)
        every.append(copies)
        if sweep == 0:
            to_rows(nbrs, nbr_rows)
            to_rows(owners, owner_rows)
        parts = blocks // 8
        per = 4

        def indices_of(f):
            return [nbr_rows[f, 8 * u : 8 * u + 8, :] for u in range(per)]

        @pl.loop(0, faces)
        def _(f):
            sums = pick(indices_of(f), zeros_8(per * comps), [(0, blocks, own(psi))], comps)
            for u in range(per):
                for c in range(comps):
                    picked[f, c, 8 * u : 8 * u + 8, :] = sums[u * comps + c]

        arrive(copies)

        def far(d):
            return lambda c, j: halo_in[sweep, d, c, pl.ds(j, 1), :]

        @pl.loop(0, faces)
        def _(f):
            before = [picked[f, c, 8 * u : 8 * u + 8, :] for u in range(per) for c in range(comps)]
            segments = [(blocks + halo_blocks * d, halo_blocks, far(d)) for d in range(4)]
            sums = pick(indices_of(f), before, segments, comps)
            for u in range(per):
                for c in range(comps):
                    picked[f, c, 8 * u : 8 * u + 8, :] = sums[u * comps + c]

        @pl.loop(0, blocks)
        def _(b):
            here = pl.ds(pl.multiple_of(b * LANES, LANES), LANES)
            acc = rhs[:, here]
            for f in range(faces):
                total = None
                for r in range(comps):
                    value = jnp.broadcast_to(picked[f, r, pl.ds(b, 1), :], (comps, LANES))
                    term = off[f, r, :, here].astype(jnp.float32) * value
                    total = term if total is None else total + term
                acc = acc - total
            new = None
            for r in range(comps):
                term = diag[r, :, here] * jnp.broadcast_to(acc[r : r + 1, :], (comps, LANES))
                new = term if new is None else new + term
            fresh[:, here] = new

    for k in (3, 2, 1, 0):
        lists = [owner_rows[k, 8 * u : 8 * u + 8, :] for u in range(per)]
        sums = pick(lists, zeros_8(per * comps), [(0, blocks, own(psi_out))], comps)
        target = owner_in.at[0] if k == 0 else owner_out.at[k - 1]
        for u in range(per):
            for c in range(comps):
                target[c, 8 * u : 8 * u + 8, :] = sums[u * comps + c]
        if k:
            copies = [remote(owner_out.at[k - 1], owner_in.at[k], 11 + k, -(k // 2), -(k % 2))]
            start(copies)
            every.append(copies)

    arrive(fine_copies)
    for c in range(comps):
        for a in range(fa):
            grown[c, a + 1, 8 : 8 + fb, :] = fine[c, a]
            grown[c, a + 1, 7:8, :] = side_in[0, c, a : a + 1, :]
            grown[c, a + 1, 8 + fb : 9 + fb, :] = side_in[1, c, a : a + 1, :]
    lane = lax.broadcasted_iota(jnp.int32, (8, LANES), 1)

    @pl.loop(0, fa)
    def _(a):
        for h in range(fb // 8):
            low = 8 + 8 * h
            laps = []
            for c in range(comps):
                mid = grown[c, a + 1, low : low + 8, :]
                beside = grown[c, a + 2, low : low + 8, :] + grown[c, a, low : low + 8, :]
                beside = beside + grown[c, a + 1, low + 1 : low + 9, :] + grown[c, a + 1, low - 1 : low + 7, :]
                beside = beside + jnp.where(lane == LANES - 1, 0.0, pltpu.roll(mid, LANES - 1, 1))
                beside = beside + jnp.where(lane == 0, 0.0, pltpu.roll(mid, 1, 1))
                laps.append(6.0 * mid - beside)
            for c in range(comps):
                total = source[c, a, 8 * h : 8 * h + 8, :]
                for k in range(comps):
                    total = total + coupling[c, k] * laps[k]
                residual[c, a, 8 * h : 8 * h + 8, :] = total

    for copies in every[SWEEPS:]:
        arrive(copies)

    halves = fb // 8

    @pl.loop(0, fa)
    def _(a):
        places = [(s, h) for s in range(2) for h in range(halves)]
        indices = [slots[s, a, 8 * h : 8 * h + 8, :] for s, h in places]

        def sent(k):
            return lambda c, j: owner_in[k, c, pl.ds(j, 1), :]

        segments = [(blocks * k, blocks, sent(k)) for k in range(4)]
        sums = pick(indices, zeros_8(len(places) * comps), segments, comps)
        for h in range(halves):
            here = slice(8 * h, 8 * h + 8)
            total = None
            for c in range(comps):
                value = weights[0, a, here, :] * sums[h * comps + c]
                value = value + weights[1, a, here, :] * sums[(halves + h) * comps + c]
                term = value * residual[c, a, here, :]
                total = term if total is None else total + term
            indicator[a, here, :] = total

    leave(fine_copies)
    for copies in every:
        leave(copies)


def on_device(peers, psi_start, rhs, off, diag, nbrs, halos, owners, slots, weights, fine, source, coupling):
    comps, cells = psi_start.shape
    faces = off.shape[0]
    blocks = cells // LANES
    halo_blocks = halos.shape[1] // LANES
    _, fa, fb, fz = fine.shape
    vmem = pl.BlockSpec(memory_space=pltpu.VMEM)
    return tuple(
        pl.pallas_call(
            functools.partial(kernel, peers),
            out_shape=(
                jax.ShapeDtypeStruct((comps, cells), jnp.float32),
                jax.ShapeDtypeStruct((fa, fb, fz), jnp.float32),
            ),
            in_specs=[vmem] * 11 + [pl.BlockSpec(memory_space=pltpu.SMEM)],
            out_specs=(vmem, vmem),
            scratch_shapes=[
                pltpu.VMEM((comps, cells), jnp.float32),
                pltpu.VMEM((faces, blocks, LANES), jnp.int32),
                pltpu.VMEM((4, halo_blocks, LANES), jnp.int32),
                pltpu.VMEM((4, blocks, LANES), jnp.int32),
                pltpu.VMEM((faces, comps, blocks, LANES), jnp.float32),
                pltpu.VMEM((SWEEPS, 4, comps, halo_blocks, LANES), jnp.float32),
                pltpu.VMEM((SWEEPS, 4, comps, halo_blocks, LANES), jnp.float32),
                pltpu.VMEM((3, comps, blocks, LANES), jnp.float32),
                pltpu.VMEM((4, comps, blocks, LANES), jnp.float32),
                pltpu.VMEM((comps, fa + 2, fb + 16, LANES), jnp.float32),
                pltpu.VMEM((2, comps, fa, LANES), jnp.float32),
                pltpu.VMEM((2, comps, fa, LANES), jnp.float32),
                pltpu.VMEM((comps, fa, fb, LANES), jnp.float32),
                pltpu.SemaphoreType.DMA((15,)),
                pltpu.SemaphoreType.DMA((15,)),
            ],
            compiler_params=pltpu.CompilerParams(
                collective_id=0, has_side_effects=True, vmem_limit_bytes=40 * 2**20
            ),
            name="indicators",
        )(psi_start, rhs, off, diag, nbrs, halos, owners, slots, weights, fine, source, coupling)
    )


def solution(mesh):
    placed = (
        P(None, ("gx", "gy")),
        P(None, ("gx", "gy")),
        P(None, None, None, ("gx", "gy")),
        P(None, None, ("gx", "gy")),
        P(None, ("gx", "gy")),
        P(None, ("gx", "gy")),
        P(None, ("gx", "gy")),
        P(None, "gx", "gy", None),
        P(None, "gx", "gy", None),
        P(None, "gx", "gy", None),
        P(None, "gx", "gy", None),
        P(),
    )
    return jax.shard_map(
        functools.partial(on_device, (mesh.shape["gx"], mesh.shape["gy"])),
        mesh=mesh,
        in_specs=placed,
        out_specs=(P(None, ("gx", "gy")), P("gx", "gy", None)),
        check_vma=False,
    )
```

time: 713 us -> 163 us (0.23)
  local copies, waits for them, and re-layouts: 629 us -> 13.2 us
  Pallas kernels: 0 us -> 148 us
  starting transfers between devices: 39.9 us -> 0 us
  other arithmetic: 18.3 us -> 0 us
  waiting for transfers between devices: 14.5 us -> 0 us
    gather x20 -> x0, local copies, waits for them, and re-layouts: 507 us -> none  [the longest x12 174 us: on_device(): values = ext[:, face_nbrs[face]]]
    pallas_call x0 -> x1, Pallas kernels: none -> 148 us  [on_device(): pl.pallas_call(functools.partial(kernel, peers), out_shape=(jax.ShapeDtyp...]
    slice x18 -> x0, local copies, waits for them, and re-layouts: 80.4 us -> none  [the longest x12 78.6 us: on_device(): acc = acc - off_blocks[face, row].astype(jnp.float32) * values[row][None]]
    ppermute x15 -> x0, starting transfers between devices: 39.9 us -> none  [the longest x11 28.3 us: passed_along(): return lax.ppermute(value, axis, pairs)]
    ppermute x15 -> x0, waiting for transfers between devices: 14.5 us -> none  [the longest x11 14.5 us: passed_along(): return lax.ppermute(value, axis, pairs)]
    unnamed x98 -> x26, local copies, waits for them, and re-layouts: 26.3 us -> 13.2 us
    concatenate x5 -> x0, local copies, waits for them, and re-layouts: 9.68 us -> none  [the longest x1 5.55 us: on_device(): received = jnp.concatenate(pieces, axis=1)]
  transfers between devices with their start and end apart: 15 -> 0, of which waited for: 4 -> 0; matrix products, arithmetic and copies ran while one was open for 53% -> 0% of each run, Pallas kernels for 0% -> 0%
where the time goes in v1:
time: 163 us; the launch traced here: 162 us
  Pallas kernels  148 us (91%)
  local copies, waits for them, and re-layouts  13.2 us (8%)
    pallas_call x1, Pallas kernels, on_device(): pl.pallas_call(functools.partial(kernel, peers), out_shape=(jax.ShapeDtyp...  148 us
    unnamed x26, local copies, waits for them, and re-layouts  13.2 us

profile of v1, /device:TPU:1, one launch (start us, length us, event | category | flops | bytes accessed | tf_op | source)
XLA Modules:
  0.0 162.3 jit_solution(14333325080327998365)
XLA Ops:
  0.6 0.0 copy-start
  0.6 1.7 %copy-done = bf16[6,6,6,4096]{3,2,1,0:T(8,128)(2,1)S(1)} copy-done((bf16[6,6,6,4096]{3,2,1,0:T(8,128)(2,1)S(1)}, bf16[6,6,6,4096]{3,2,1,0:T(8,128)(2,1)}, u32[]{:S(2)}) %copy-start) | copy-done | bytes 1769496
  2.3 0.0 copy-start.1
  2.3 1.1 copy-done.1
  3.4 0.0 copy-start.2
  3.4 1.1 copy-done.2
  4.6 0.0 copy-start.3
  4.6 1.1 copy-done.3
  5.7 0.0 copy-start.4
  5.7 0.9 copy-done.4
  6.7 0.0 copy-start.5
  6.7 0.9 copy-done.5
  7.6 0.0 copy-start.6
  7.6 0.9 copy-done.6
  8.5 0.0 copy-start.7
  8.5 0.9 copy-done.7
  9.4 0.0 copy-start.8
  9.4 0.9 copy-done.8
  10.3 0.0 copy-start.9
  10.3 0.8 copy-done.9
  11.2 0.0 copy-start.10
  11.2 0.7 copy-done.10
  11.9 0.0 copy-start.11
  11.9 0.7 copy-done.11
  12.6 148.4 %indicators.1 = (f32[6,4096]{1,0:T(8,128)S(1)}, f32[16,16,128]{2,1,0:T(8,128)S(1)}) custom-call(f32[6,4096]{1,0:T(8,128)S(1)} %copy-done.6, f32[6,4096]{1,0:T(8,128)S(1)} %copy-done.7, bf16[6,6,6,4096]{3,2,1,0:T(8,128)(2,1)S(1)} %copy-done, f32[6,6,4096]{2,1,0:T(8,128)S(1)} %copy-done.1, s32[6,4096]{1,0:T(8,128)S(1)} %copy-done.8, s32[4,1024]{1,0:T(4,128)S(1)} %copy-done.10, ...), custom_call_target="tpu_custom_call" | custom-call | tf_op jit(solution)/shard_map/indicators/pallas_call | solution.py:295
  161.0 0.7 copy.16
  161.7 0.7 copy.17
Async XLA Ops:
  0.6 1.7 %copy-start = (bf16[6,6,6,4096]{3,2,1,0:T(8,128)(2,1)S(1)}, bf16[6,6,6,4096]{3,2,1,0:T(8,128)(2,1)}, u32[]{:S(2)}) copy-start(bf16[6,6,6,4096]{3,2,1,0:T(8,128)(2,1)} %off.1) | copy-start | bytes 5308420
  2.3 1.1 copy-start.1
  3.4 1.1 copy-start.2
  4.6 1.1 copy-start.3
  5.7 0.9 copy-start.4
  6.7 0.9 copy-start.5
  7.6 0.9 copy-start.6
  8.5 0.9 copy-start.7
  9.4 0.9 copy-start.8
  10.3 0.8 copy-start.9
  11.2 0.7 copy-start.10
  11.9 0.7 copy-start.11

commit v2 on v1

--- a/solution.py
+++ b/solution.py
@@ -9,6 +9,7 @@
 
 SWEEPS = 2
 LANES = 128
+LEVELS = 32767.0
 MESH = pl.DeviceIdType.MESH
 
 
@@ -23,26 +24,48 @@
             dst[k, j : j + 1, :] = src[k : k + 1, j * LANES : (j + 1) * LANES]
 
 
-def pick(indices, totals, segments, comps, unroll=8):
-    lanes = [index & (LANES - 1) for index in indices]
-    rows = [index >> 7 for index in indices]
-    for first, count, load in segments:
-
-        def step(j, totals):
-            values = [jnp.broadcast_to(load(c, j), (8, LANES)) for c in range(comps)]
-            out = []
-            for u in range(len(indices)):
-                here = rows[u] == first + j
+def pick(indices, totals, segments, comps):
+    totals = list(totals)
+    for u, index in enumerate(indices):
+        lanes, rows = index & (LANES - 1), index >> 7
+        for first, count, load in segments:
+            for j in range(count):
+                here = rows == first + j
                 for c in range(comps):
-                    out.append(jnp.where(here, lane_take(values[c], lanes[u]), totals[u * comps + c]))
-            return tuple(out)
-
-        totals = lax.fori_loop(0, count, step, tuple(totals), unroll=min(unroll, count))
+                    value = jnp.broadcast_to(load(c, j), (8, LANES))
+                    at = u * comps + c
+                    totals[at] = jnp.where(here, lane_take(value, lanes), totals[at])
     return totals
 
 
-def zeros_8(count):
-    return [jnp.zeros((8, LANES), jnp.float32) for _ in range(count)]
+def zeros_8(count, dtype=jnp.float32):
+    return [jnp.zeros((8, LANES), dtype) for _ in range(count)]
+
+
+def peak_of(values):
+    return jnp.maximum(jnp.max(jnp.abs(values)), 1e-30)
+
+
+def coded(value, scale):
+    root = jnp.sqrt(jnp.sqrt(jnp.abs(value) * scale)) * LEVELS + 0.5
+    return jnp.where(value < 0.0, -root, root).astype(jnp.int32)
+
+
+def pair_coded(first, second, peak):
+    scale = 1.0 / peak
+    return coded(first, scale) * 65536 + coded(second, scale)
+
+
+def decoded(code, peak):
+    root = code.astype(jnp.float32) * (1.0 / LEVELS)
+    square = root * root
+    value = square * square * peak
+    return jnp.where(code < 0, -value, value)
+
+
+def pair_decoded(word, peak):
+    first = (word + 32768) >> 16
+    return decoded(first, peak), decoded(word - first * 65536, peak)
 
 
 def kernel(
@@ -74,10 +97,14 @@
     side_out,
     side_in,
     residual,
+    own_words,
+    far_words,
+    parent_words,
     send_sem,
     recv_sem,
 ):
     comps, cells = psi_start.shape
+    pairs = comps // 2
     faces = off.shape[0]
     blocks = cells // LANES
     halo_blocks = halo_rows.shape[1]
@@ -153,7 +180,7 @@
     to_rows(halos, halo_rows)
 
     def own(ref):
-        return lambda c, j: ref[c : c + 1, pl.ds(pl.multiple_of(j * LANES, LANES), LANES)]
+        return lambda c, j: ref[c : c + 1, j * LANES : (j + 1) * LANES]
 
     every = []
     for sweep in range(SWEEPS):
@@ -178,26 +205,35 @@
         def indices_of(f):
             return [nbr_rows[f, 8 * u : 8 * u + 8, :] for u in range(per)]
 
+        peak = peak_of(psi[...])
+        own_words[...] = pair_coded(psi[0:pairs, :], psi[pairs:comps, :], peak)
+
         @pl.loop(0, faces)
         def _(f):
-            sums = pick(indices_of(f), zeros_8(per * comps), [(0, blocks, own(psi))], comps)
+            sums = pick(indices_of(f), zeros_8(per * pairs, jnp.int32), [(0, blocks, own(own_words))], pairs)
             for u in range(per):
-                for c in range(comps):
-                    picked[f, c, 8 * u : 8 * u + 8, :] = sums[u * comps + c]
+                for c in range(pairs):
+                    first, second = pair_decoded(sums[u * pairs + c], peak)
+                    picked[f, c, 8 * u : 8 * u + 8, :] = first
+                    picked[f, c + pairs, 8 * u : 8 * u + 8, :] = second
 
         arrive(copies)
+        far_peak = peak_of(halo_in[sweep])
+        far_words[...] = pair_coded(halo_in[sweep, :, 0:pairs], halo_in[sweep, :, pairs:comps], far_peak)
 
         def far(d):
-            return lambda c, j: halo_in[sweep, d, c, pl.ds(j, 1), :]
+            return lambda c, j: far_words[d, c, j : j + 1, :]
 
         @pl.loop(0, faces)
         def _(f):
-            before = [picked[f, c, 8 * u : 8 * u + 8, :] for u in range(per) for c in range(comps)]
             segments = [(blocks + halo_blocks * d, halo_blocks, far(d)) for d in range(4)]
-            sums = pick(indices_of(f), before, segments, comps)
+            sums = pick(indices_of(f), zeros_8(per * pairs, jnp.int32), segments, pairs)
             for u in range(per):
-                for c in range(comps):
-                    picked[f, c, 8 * u : 8 * u + 8, :] = sums[u * comps + c]
+                rows = slice(8 * u, 8 * u + 8)
+                for c in range(pairs):
+                    first, second = pair_decoded(sums[u * pairs + c], far_peak)
+                    picked[f, c, rows, :] = picked[f, c, rows, :] + first
+                    picked[f, c + pairs, rows, :] = picked[f, c + pairs, rows, :] + second
 
         @pl.loop(0, blocks)
         def _(b):
@@ -258,17 +294,25 @@
         arrive(copies)
 
     halves = fb // 8
+    parent_peak = peak_of(owner_in[...])
+
+    @pl.loop(0, 4)
+    def _(k):
+        parent_words[k] = pair_coded(owner_in[k, 0:pairs], owner_in[k, pairs:comps], parent_peak)
 
     @pl.loop(0, fa)
     def _(a):
         places = [(s, h) for s in range(2) for h in range(halves)]
         indices = [slots[s, a, 8 * h : 8 * h + 8, :] for s, h in places]
 
-        def sent(k):
-            return lambda c, j: owner_in[k, c, pl.ds(j, 1), :]
-
-        segments = [(blocks * k, blocks, sent(k)) for k in range(4)]
-        sums = pick(indices, zeros_8(len(places) * comps), segments, comps)
+        def sent(k, sums):
+            return tuple(pick(indices, sums, [(blocks * k, blocks, lambda c, j: parent_words[k, c, j : j + 1, :])], pairs))
+
+        words = lax.fori_loop(0, 4, sent, tuple(zeros_8(len(places) * pairs, jnp.int32)))
+        sums = [None] * (len(places) * comps)
+        for u in range(len(places)):
+            for c in range(pairs):
+                sums[u * comps + c], sums[u * comps + c + pairs] = pair_decoded(words[u * pairs + c], parent_peak)
         for h in range(halves):
             here = slice(8 * h, 8 * h + 8)
             total = None
@@ -314,6 +358,9 @@
                 pltpu.VMEM((2, comps, fa, LANES), jnp.float32),
                 pltpu.VMEM((2, comps, fa, LANES), jnp.float32),
                 pltpu.VMEM((comps, fa, fb, LANES), jnp.float32),
+                pltpu.VMEM((comps // 2, cells), jnp.int32),
+                pltpu.VMEM((4, comps // 2, halo_blocks, LANES), jnp.int32),
+                pltpu.VMEM((4, comps // 2, blocks, LANES), jnp.int32),
                 pltpu.SemaphoreType.DMA((15,)),
                 pltpu.SemaphoreType.DMA((15,)),
             ],

time: 163 us -> 76.5 us (0.47)
  Pallas kernels: 148 us -> 61.9 us
    pallas_call x1, Pallas kernels: 148 us -> 61.9 us  [on_device(): pl.pallas_call(functools.partial(kernel, peers), out_shape=(jax.ShapeDtyp...]
where the time goes in v2:
time: 76.5 us; the launch traced here: 75.8 us
  Pallas kernels  61.9 us (81%)
  local copies, waits for them, and re-layouts  13.2 us (17%)
    pallas_call x1, Pallas kernels, on_device(): pl.pallas_call(functools.partial(kernel, peers), out_shape=(jax.ShapeDtyp...  61.9 us
    unnamed x26, local copies, waits for them, and re-layouts  13.2 us

profile of v2, /device:TPU:1, one launch (start us, length us, event | category | flops | bytes accessed | tf_op | source)
XLA Modules:
  0.0 75.8 jit_solution(18027183911310210060)
XLA Ops:
  0.6 0.0 copy-start
  0.6 1.7 %copy-done = bf16[6,6,6,4096]{3,2,1,0:T(8,128)(2,1)S(1)} copy-done((bf16[6,6,6,4096]{3,2,1,0:T(8,128)(2,1)S(1)}, bf16[6,6,6,4096]{3,2,1,0:T(8,128)(2,1)}, u32[]{:S(2)}) %copy-start) | copy-done | bytes 1769496
  2.3 0.0 copy-start.1
  2.3 1.1 %copy-done.1 = f32[6,6,4096]{2,1,0:T(8,128)S(1)} copy-done((f32[6,6,4096]{2,1,0:T(8,128)S(1)}, f32[6,6,4096]{2,1,0:T(8,128)}, u32[]{:S(2)}) %copy-start.1) | copy-done | bytes 589848
  3.4 0.0 copy-start.2
  3.4 1.1 %copy-done.2 = f32[6,16,16,128]{3,2,1,0:T(8,128)S(1)} copy-done((f32[6,16,16,128]{3,2,1,0:T(8,128)S(1)}, f32[6,16,16,128]{3,2,1,0:T(8,128)}, u32[]{:S(2)}) %copy-start.2) | copy-done | bytes 786456
  4.6 0.0 copy-start.3
  4.6 1.1 %copy-done.3 = f32[6,16,16,128]{3,2,1,0:T(8,128)S(1)} copy-done((f32[6,16,16,128]{3,2,1,0:T(8,128)S(1)}, f32[6,16,16,128]{3,2,1,0:T(8,128)}, u32[]{:S(2)}) %copy-start.3) | copy-done | bytes 786456
  5.7 0.0 copy-start.4
  5.7 0.9 %copy-done.4 = s32[2,16,16,128]{3,2,1,0:T(8,128)S(1)} copy-done((s32[2,16,16,128]{3,2,1,0:T(8,128)S(1)}, s32[2,16,16,128]{3,2,1,0:T(8,128)}, u32[]{:S(2)}) %copy-start.4) | copy-done | bytes 262168
  6.7 0.0 copy-start.5
  6.7 0.9 %copy-done.5 = f32[2,16,16,128]{3,2,1,0:T(8,128)S(1)} copy-done((f32[2,16,16,128]{3,2,1,0:T(8,128)S(1)}, f32[2,16,16,128]{3,2,1,0:T(8,128)}, u32[]{:S(2)}) %copy-start.5) | copy-done | bytes 262168
  7.6 0.0 copy-start.6
  7.6 0.9 %copy-done.6 = f32[6,4096]{1,0:T(8,128)S(1)} copy-done((f32[6,4096]{1,0:T(8,128)S(1)}, f32[6,4096]{1,0:T(8,128)}, u32[]{:S(2)}) %copy-start.6) | copy-done | bytes 98328
  8.5 0.0 copy-start.7
  8.5 0.9 %copy-done.7 = f32[6,4096]{1,0:T(8,128)S(1)} copy-done((f32[6,4096]{1,0:T(8,128)S(1)}, f32[6,4096]{1,0:T(8,128)}, u32[]{:S(2)}) %copy-start.7) | copy-done | bytes 98328
  9.4 0.0 copy-start.8
  9.4 0.9 %copy-done.8 = s32[6,4096]{1,0:T(8,128)S(1)} copy-done((s32[6,4096]{1,0:T(8,128)S(1)}, s32[6,4096]{1,0:T(8,128)}, u32[]{:S(2)}) %copy-start.8) | copy-done | bytes 98328
  10.3 0.0 copy-start.9
  10.3 0.8 %copy-done.9 = s32[4,4096]{1,0:T(4,128)S(1)} copy-done((s32[4,4096]{1,0:T(4,128)S(1)}, s32[4,4096]{1,0:T(4,128)}, u32[]{:S(2)}) %copy-start.9) | copy-done | bytes 65560
  11.2 0.0 copy-start.10
  11.2 0.7 copy-done.10
  11.9 0.0 copy-start.11
  11.9 0.7 copy-done.11
  12.6 61.9 %indicators.1 = (f32[6,4096]{1,0:T(8,128)S(1)}, f32[16,16,128]{2,1,0:T(8,128)S(1)}) custom-call(f32[6,4096]{1,0:T(8,128)S(1)} %copy-done.6, f32[6,4096]{1,0:T(8,128)S(1)} %copy-done.7, bf16[6,6,6,4096]{3,2,1,0:T(8,128)(2,1)S(1)} %copy-done, f32[6,6,4096]{2,1,0:T(8,128)S(1)} %copy-done.1, s32[6,4096]{1,0:T(8,128)S(1)} %copy-done.8, s32[4,1024]{1,0:T(4,128)S(1)} %copy-done.10, ...), custom_call_target="tpu_custom_call" | custom-call | tf_op jit(solution)/shard_map/indicators/pallas_call | solution.py:339
  74.5 0.7 copy.16
  75.1 0.7 copy.17
Async XLA Ops:
  0.6 1.7 %copy-start = (bf16[6,6,6,4096]{3,2,1,0:T(8,128)(2,1)S(1)}, bf16[6,6,6,4096]{3,2,1,0:T(8,128)(2,1)}, u32[]{:S(2)}) copy-start(bf16[6,6,6,4096]{3,2,1,0:T(8,128)(2,1)} %off.1) | copy-start | bytes 5308420
  2.3 1.1 %copy-start.1 = (f32[6,6,4096]{2,1,0:T(8,128)S(1)}, f32[6,6,4096]{2,1,0:T(8,128)}, u32[]{:S(2)}) copy-start(f32[6,6,4096]{2,1,0:T(8,128)} %diag.1) | copy-start | bytes 1769476
  3.4 1.1 %copy-start.2 = (f32[6,16,16,128]{3,2,1,0:T(8,128)S(1)}, f32[6,16,16,128]{3,2,1,0:T(8,128)}, u32[]{:S(2)}) copy-start(f32[6,16,16,128]{3,2,1,0:T(8,128)} %fine.1) | copy-start | bytes 2359300
  4.6 1.1 %copy-start.3 = (f32[6,16,16,128]{3,2,1,0:T(8,128)S(1)}, f32[6,16,16,128]{3,2,1,0:T(8,128)}, u32[]{:S(2)}) copy-start(f32[6,16,16,128]{3,2,1,0:T(8,128)} %source.1) | copy-start | bytes 2359300
  5.7 0.9 %copy-start.4 = (s32[2,16,16,128]{3,2,1,0:T(8,128)S(1)}, s32[2,16,16,128]{3,2,1,0:T(8,128)}, u32[]{:S(2)}) copy-start(s32[2,16,16,128]{3,2,1,0:T(8,128)} %slots.1) | copy-start | bytes 786436
  6.7 0.9 %copy-start.5 = (f32[2,16,16,128]{3,2,1,0:T(8,128)S(1)}, f32[2,16,16,128]{3,2,1,0:T(8,128)}, u32[]{:S(2)}) copy-start(f32[2,16,16,128]{3,2,1,0:T(8,128)} %weights.1) | copy-start | bytes 786436
  7.6 0.9 %copy-start.6 = (f32[6,4096]{1,0:T(8,128)S(1)}, f32[6,4096]{1,0:T(8,128)}, u32[]{:S(2)}) copy-start(f32[6,4096]{1,0:T(8,128)} %psi_start.1) | copy-start | bytes 294916
  8.5 0.9 %copy-start.7 = (f32[6,4096]{1,0:T(8,128)S(1)}, f32[6,4096]{1,0:T(8,128)}, u32[]{:S(2)}) copy-start(f32[6,4096]{1,0:T(8,128)} %rhs.1) | copy-start | bytes 294916
  9.4 0.9 %copy-start.8 = (s32[6,4096]{1,0:T(8,128)S(1)}, s32[6,4096]{1,0:T(8,128)}, u32[]{:S(2)}) copy-start(s32[6,4096]{1,0:T(8,128)} %nbrs.1) | copy-start | bytes 294916
  10.3 0.8 %copy-start.9 = (s32[4,4096]{1,0:T(4,128)S(1)}, s32[4,4096]{1,0:T(4,128)}, u32[]{:S(2)}) copy-start(s32[4,4096]{1,0:T(4,128)} %owners.1) | copy-start | bytes 196612
  11.2 0.7 copy-start.10
  11.9 0.7 copy-start.11
